TPU v7x, 512 devices: a whole 4x8x8 slice. The times are simulated.
512 devices in a mesh: gx: 4 (over x_hi, core), gy: 16 (over x_lo, y), ma: 8 (over z).
Axes of the slice: x: 4 (x_hi: 2, x_lo: 2; x = x_hi * 2 + x_lo), y: 8, z: 8, core: 2. Of those that a mesh axis runs over, the one named last changes fastest.
Arguments:
- spectra: bfloat16 [64, 2048, 2048], P('gx', 'gy', 'ma'), as said below
- loadings: float32 [32, 64, 2048], P(None, 'gx', 'gy'), as said below
- profiles: float32 [32, 2048], P(None, 'ma'), may hold values from 0.5 to 2
Outputs:
- new_load: float32 [32, 64, 2048], P(None, 'gx', 'gy')
- new_prof: float32 [32, 2048], P(None, 'ma')
Inputs may be any that keep to these rules, and one draw needn't show every extreme that they name: `spectra`: positive. `loadings`: positive.
All inputs are finite; a program needn't handle non-finite values.
Results may differ from a plain program's by a relative error of at most 0.0003.
Values may be sent and summed in bfloat16 or wider, within the bound.
A program may use at most 64 MiB of HBM per device.

v0:
```python
import jax
import jax.numpy as jnp
from jax import lax
from jax.sharding import PartitionSpec as P

M = 2048
RADIUS = 2


epsilon = 1e-06


def extended(block, sides, width):
    for axis, dim in sides:
        count = lax.axis_size(axis)
        forward = [(i, i + 1) for i in range(count - 1)]
        backward = [(target, source) for source, target in forward]
        low = lax.ppermute(
            lax.slice_in_dim(block, block.shape[dim] - width, None, axis=dim), axis, forward
        )
        high = lax.ppermute(lax.slice_in_dim(block, 0, width, axis=dim), axis, backward)
        block = jnp.concatenate([low, block, high], axis=dim)
    return block


def kernel_taps():
    offsets = jnp.arange(-RADIUS, RADIUS + 1).astype(jnp.float32)
    raw = jnp.exp(-offsets * offsets / 2.0)
    return raw / jnp.sum(raw)


def smooth_dim(padded, dim, count):
    taps = kernel_taps()
    total = None
    for offset in range(2 * RADIUS + 1):
        term = taps[offset] * lax.slice_in_dim(padded, offset, offset + count, axis=dim)
        total = term if total is None else total + term
    return total


def per_device(spectra, loadings, profiles):
    high = lax.Precision.HIGHEST
    rows_x = spectra.shape[0]
    rows_y = spectra.shape[1]
    padded = extended(spectra, (("gx", 0),), RADIUS)
    along_x = smooth_dim(padded.astype(jnp.float32), 0, rows_x)
    padded_y = extended(along_x, (("gy", 1),), RADIUS)
    smoothed = smooth_dim(padded_y, 1, rows_y)
    partial_bg = jnp.sum(smoothed, axis=2)
    background = lax.psum(partial_bg, "ma") / M
    cleaned = jnp.maximum(smoothed - background[:, :, None], 0.0)
    numer_part = jnp.einsum("kxy,xym->km", loadings, cleaned, precision=high)
    gram_part = jnp.einsum("kxy,jxy->kj", loadings, loadings, precision=high)
    numer_prof, gram_load = lax.psum((numer_part, gram_part), ("gx", "gy"))
    new_prof = profiles * numer_prof / (jnp.dot(gram_load, profiles, precision=high) + epsilon)
    numer_local = jnp.einsum("km,xym->kxy", new_prof, cleaned, precision=high)
    gram_local = jnp.dot(new_prof, new_prof.T, precision=high)
    numer_load, gram_prof = lax.psum((numer_local, gram_local), "ma")
    below = jnp.einsum("kj,jxy->kxy", gram_prof, loadings, precision=high) + epsilon
    new_load = loadings * numer_load / below
    return (new_load, new_prof)


def solution(mesh):
    placed = (P("gx", "gy", "ma"), P(None, "gx", "gy"), P(None, "ma"))
    return jax.shard_map(
        per_device,
        mesh=mesh,
        in_specs=placed,
        out_specs=(P(None, "gx", "gy"), P(None, "ma")),
        check_vma=False,
    )
```

profile of v0, /device:TPU:1, one launch (start us, length us, event | category | flops | bytes accessed | tf_op | source)
XLA Modules:
  0.0 385.3 jit_solution(14095044977622310725)
XLA Ops:
  7.2 0.0 all-reduce.3.cloned.1.call-start
  7.2 1.0 fusion.34
  8.2 6.0 %collective-permute-start = (bf16[2,128,256]{2,1,0:T(8,128)(2,1)S(1)}, bf16[2,128,256]{2,1,0:T(8,128)(2,1)S(1)}, u32[]{:S(2)}, u32[]{:S(2)}) collective-permute-start(bf16[2,128,256]{2,1,0:T(8,128)(2,1)S(1)} %get-tuple-element.10), channel_id=1, source_target_pairs={{0,128},{128,256},{256,384},{1,129},{129,257},{257,385},{2,130},{1... | collective-permute-start | bytes 393224 | tf_op jit(solution)/shard_map/ppermute | solution.py:18
  14.3 4.0 %collective-permute-start.1 = (bf16[2,128,256]{2,1,0:T(8,128)(2,1)S(1)}, bf16[2,128,256]{2,1,0:T(8,128)(2,1)S(1)}, u32[]{:S(2)}, u32[]{:S(2)}) collective-permute-start(bf16[2,128,256]{2,1,0:T(8,128)(2,1)S(1)} %get-tuple-element.11), channel_id=1, source_target_pairs={{128,0},{256,128},{384,256},{129,1},{257,129},{385,257},{130,2},{2... | collective-permute-start | bytes 393224 | tf_op jit(solution)/shard_map/ppermute | solution.py:21
  18.3 0.6 fusion.28
  18.9 0.7 broadcast_divide_fusion
  19.6 0.7 fusion.35
  20.2 0.0 collective-permute-done
  20.3 1.8 collective-permute-done.1
  22.0 1.4 maximum_convert_fusion
  23.5 0.0 copy-start
  23.5 3.8 fusion.10
  27.3 3.2 collective-permute-start.2
  30.6 1.3 collective-permute-start.3
  31.9 0.0 copy-done
  31.9 0.4 convolution_bitcast_fusion
  32.3 0.0 collective-permute-done.2
  32.3 2.9 collective-permute-done.3
  35.2 4.7 %fusion.31 = (f32[16,128]{1,0:T(8,128)S(1)}, f32[16,128,256]{2,1,0:T(8,128)S(1)}) fusion(f32[16,2,256]{2,1,0:T(2,128)S(1)} %collective-permute-done.3, f32[16,128,256]{2,1,0:T(8,128)S(1)} %fusion.10, f32[]{:T(128)} %bitcast.4, f32[]{:T(128)} %bitcast.3, f32[]{:T(128)} %bitcast.2, f32[16,2,256]{2,1,0:T(2,128)S(1)} %collective-permute-done.2, f32[]{:T(128)} %bitcast.1, ...), kind=kLoop, calls=%fused_computation.52 | loop fusion | flops 7337984 | bytes 4268052 | tf_op jit(solution)/shard_map/reduce_sum | solution.py:49
  40.0 0.0 copy-start.2
  40.0 20.0 %psum.35 = f32[16,128]{1,0:T(8,128)S(1)} all-reduce(f32[16,128]{1,0:T(8,128)S(1)} %get-tuple-element.6), channel_id=1, replica_groups=mesh['gx'=4,'gy'=16,'ma'=8] {'ma'}, use_global_device_ids=true, to_apply=%region_2.0 | all-reduce | flops 2048 | bytes 16384 | tf_op jit(solution)/shard_map/psum | solution.py:50
  60.0 1.5 fusion.16
  61.5 232.5 %all-reduce = (f32[32,32]{1,0:T(8,128)S(1)}, f32[32,256]{1,0:T(8,128)S(1)}) all-reduce(f32[32,32]{1,0:T(8,128)S(1)} %convolution_bitcast_fusion, f32[32,256]{1,0:T(8,128)S(1)} %fusion.16), channel_id=1, replica_groups=mesh['gx'=4,'gy'=16,'ma'=8] {'gx','gy'}, use_global_device_ids=true, to_apply=%region_4.0 | all-reduce | flops 9216 | bytes 73728 | tf_op jit(solution)/shard_map/psum | solution.py:54
  294.0 0.0 copy-done.2
  294.0 0.2 multiply_divide_fusion.1
  294.2 0.0 copy-start.1
  294.2 2.8 fusion.14
  297.0 0.0 all-reduce.3.cloned.1.call-update
  297.0 0.2 fusion.36
  297.2 20.7 %psum.39 = f32[32,32]{1,0:T(8,128)S(1)} all-reduce(f32[32,32]{1,0:T(8,128)S(1)} %fusion.36), channel_id=1, replica_groups=mesh['gx'=4,'gy'=16,'ma'=8] {'ma'}, use_global_device_ids=true, to_apply=%region_6.0 | all-reduce | flops 1024 | bytes 8192 | tf_op jit(solution)/shard_map/psum | solution.py:58
  317.8 0.4 convolution_add_fusion
  318.3 58.3 %all-reduce.3.cloned.1.call-done = f32[32,16,128]{2,0,1:T(8,128)} async-done(((f32[32,16,128]{2,0,1:T(8,128)}), f32[32,16,128]{2,0,1:T(8,128)}) %all-reduce.3.cloned.1.call-update) | async-done | bytes 262160 | tf_op jit(solution)/shard_map/psum | solution.py:58
  376.6 1.1 multiply_divide_fusion
  377.6 0.0 copy-done.1
  377.6 0.9 copy.8
  (2 shorter events, 0.0 us)
Async XLA Ops:
  7.2 369.4 %all-reduce.3.cloned.1.call-start = ((), (), s32[]{:S(2)}) async-start(), calls=%async_computation | async-start | bytes 524288 | tf_op jit(solution)/shard_map/psum | solution.py:58
  8.2 12.0 %collective-permute-start = (bf16[2,128,256]{2,1,0:T(8,128)(2,1)S(1)}, bf16[2,128,256]{2,1,0:T(8,128)(2,1)S(1)}, u32[]{:S(2)}, u32[]{:S(2)}) collective-permute-start(bf16[2,128,256]{2,1,0:T(8,128)(2,1)S(1)} %get-tuple-element.10), channel_id=1, source_target_pairs={{0,128},{128,256},{256,384},{1,129},{129,257},{257,385},{2,130},{1... | collective-permute-start | bytes 393224 | tf_op jit(solution)/shard_map/ppermute | solution.py:18
  14.3 7.8 %collective-permute-start.1 = (bf16[2,128,256]{2,1,0:T(8,128)(2,1)S(1)}, bf16[2,128,256]{2,1,0:T(8,128)(2,1)S(1)}, u32[]{:S(2)}, u32[]{:S(2)}) collective-permute-start(bf16[2,128,256]{2,1,0:T(8,128)(2,1)S(1)} %get-tuple-element.11), channel_id=1, source_target_pairs={{128,0},{256,128},{384,256},{129,1},{257,129},{385,257},{130,2},{2... | collective-permute-start | bytes 393224 | tf_op jit(solution)/shard_map/ppermute | solution.py:21
  23.5 8.4 %copy-start = (f32[32,16,128]{2,1,0:T(8,128)S(1)}, f32[32,16,128]{2,1,0:T(8,128)}, u32[]{:S(2)}) copy-start(f32[32,16,128]{2,1,0:T(8,128)} %param.4) | copy-start | bytes 786436
  27.3 4.9 %collective-permute-start.2 = (f32[16,2,256]{2,1,0:T(2,128)S(1)}, f32[16,2,256]{2,1,0:T(2,128)S(1)}, u32[]{:S(2)}, u32[]{:S(2)}) collective-permute-start(f32[16,2,256]{2,1,0:T(2,128)S(1)} %get-tuple-element.8), channel_id=1, source_target_pairs={{0,8},{8,16},{16,24},{24,32},{32,40},{40,48},{48,56},{56,64},{64,7... | collective-permute-start | bytes 98312 | tf_op jit(solution)/shard_map/ppermute | solution.py:18
  30.6 4.7 %collective-permute-start.3 = (f32[16,2,256]{2,1,0:T(2,128)S(1)}, f32[16,2,256]{2,1,0:T(2,128)S(1)}, u32[]{:S(2)}, u32[]{:S(2)}) collective-permute-start(f32[16,2,256]{2,1,0:T(2,128)S(1)} %get-tuple-element.9), channel_id=1, source_target_pairs={{8,0},{16,8},{24,16},{32,24},{40,32},{48,40},{56,48},{64,56},{72,6... | collective-permute-start | bytes 98312 | tf_op jit(solution)/shard_map/ppermute | solution.py:21
  40.0 254.1 %copy-start.2 = (f32[32,256]{1,0:T(8,128)S(1)}, f32[32,256]{1,0:T(8,128)}, u32[]{:S(2)}) copy-start(f32[32,256]{1,0:T(8,128)} %param.5) | copy-start | bytes 98308
  294.2 83.4 %copy-start.1 = (f32[32,256]{1,0:T(8,128)}, f32[32,256]{1,0:T(8,128)S(1)}, u32[]{:S(2)}) copy-start(f32[32,256]{1,0:T(8,128)S(1)} %multiply_divide_fusion.1) | copy-start | bytes 98308
Sparse Core Ops, SparseCore 0:
  297.1 79.3 all-reduce.2
where the time goes:
time: 390 us; the launch traced here: 385 us
  blocking collectives  273 us (70%)
  waiting for transfers between devices  63 us (16%)
  starting transfers between devices  14.6 us (4%)
  between operations  14.2 us (4%)
  other arithmetic  12.3 us (3%)
  matrix products  5.39 us (1%)
    psum x1, blocking collectives, per_device(): numer_prof, gram_load = lax.psum((numer_part, gram_part), ('gx', 'gy'))  233 us
    psum x1, waiting for transfers between devices, per_device(): numer_load, gram_prof = lax.psum((numer_local, gram_local), 'ma')  58.3 us
    psum x1, blocking collectives, per_device(): numer_load, gram_prof = lax.psum((numer_local, gram_local), 'ma')  20.7 us
    psum x1, blocking collectives, per_device(): background = lax.psum(partial_bg, 'ma') / M  20 us
    ppermute x2, starting transfers between devices, extended(): lax.ppermute(lax.slice_in_dim(block, block.shape[dim] - width, None, axis...  9.24 us
  transfers between devices with their start and end apart: 5, of which 3 were waited for; matrix products, arithmetic and copies ran while one was open for 1% of the time, Pallas kernels for 0%

commit v1 on v0

v1 whole, which is shorter than its diff:
```python
import functools

import jax
import jax.numpy as jnp
import ml_dtypes
import numpy as np
from jax import lax
from jax.experimental import pallas as pl
from jax.experimental.pallas import tpu as pltpu
from jax.sharding import PartitionSpec as P

MESH = pl.DeviceIdType.MESH
F32 = jnp.float32
BF16 = jnp.bfloat16
HIGH = lax.Precision.HIGHEST

RADIUS = 2
SIDE = 16
GROUP = 8
EPSILON = 1e-06
ORDER = (4, 3, 5, 2, 6, 1, 7)

NT = (((1,), (1,)), ((), ()))
NN = (((1,), (0,)), ((), ()))


def taps():
    offsets = np.arange(-RADIUS, RADIUS + 1).astype(np.float32)
    raw = np.exp(-offsets * offsets / np.float32(2.0))
    return (raw / np.sum(raw)).astype(np.float32)


def split(value):
    high = value.astype(BF16)
    return high, (value - high.astype(F32)).astype(BF16)


def dot(a, b, dims, precision=None):
    return lax.dot_general(a, b, dims, precision=precision, preferred_element_type=F32)


def band(shape, shift, weights):
    row = lax.broadcasted_iota(jnp.int32, shape, 0)
    column = lax.broadcasted_iota(jnp.int32, shape, 1)
    at = column - row - shift
    out = jnp.zeros(shape, F32)
    for a in range(-RADIUS, RADIUS + 1):
        out = jnp.where(at == a, float(weights[a + RADIUS]), out)
    return out


def block_mask(b):
    lane = lax.broadcasted_iota(jnp.int32, (8, 128), 1)
    return jnp.logical_and(lane >= 32 * b, lane < 32 * (b + 1))


def pack_gram(full):
    out = jnp.zeros((8, 128), F32)
    for b in range(4):
        out = jnp.where(block_mask(b), full[8 * b:8 * b + 8, :], out)
    return out


def unpack_gram(packed):
    return jnp.concatenate([jnp.where(block_mask(b), packed, 0.0) for b in range(4)], axis=0)


def kernel(
    spectra, loadings, profiles, out_load, out_prof,
    ext, load_in, prof_in, ysm, smooth, rows, load_flat, load_split, clean_hi, clean_lo,
    bg_all, gram_a, gram_b, prof_send, prof_1, prof_2, prof_3, prof_new,
    gram_c, part_send, part_all, new_all, pad_t,
    local_sem, halo_send, halo_recv, send_sem, recv_sem,
):
    nx = spectra.shape[0]
    ny = spectra.shape[1]
    gx, gy, ma = lax.axis_index("gx"), lax.axis_index("gy"), lax.axis_index("ma")
    count_x, count_y = lax.axis_size("gx"), lax.axis_size("gy")
    half, y = gy // GROUP, gy % GROUP
    xc = gx * 2 + half
    weights = taps()

    def z_peer(p):
        return {"gx": gx, "gy": gy, "ma": p}

    def y_peer(p):
        return {"gx": gx, "gy": half * GROUP + p, "ma": ma}

    def xc_peer(p):
        return {"gx": p // 2, "gy": (p % 2) * GROUP + y, "ma": ma}

    copy_spectra = pltpu.make_async_copy(
        spectra, ext.at[RADIUS:RADIUS + nx, SIDE:SIDE + ny, :], local_sem.at[0]
    )
    copy_load = pltpu.make_async_copy(loadings, load_in, local_sem.at[1])
    copy_prof = pltpu.make_async_copy(profiles, prof_in, local_sem.at[2])
    copy_load.start()
    copy_spectra.start()
    copy_prof.start()

    has = {
        ("x", -1): gx > 0, ("x", 0): None, ("x", 1): gx < count_x - 1,
        ("y", -1): gy > 0, ("y", 0): None, ("y", 1): gy < count_y - 1,
    }
    steps = [(0, -1), (0, 1), (-1, 0), (1, 0), (-1, -1), (-1, 1), (1, -1), (1, 1)]

    def exists(dx, dy):
        a, b = has[("x", dx)], has[("y", dy)]
        if a is None:
            return b
        if b is None:
            return a
        return jnp.logical_and(a, b)

    send_x = {-1: slice(0, RADIUS), 0: slice(0, nx), 1: slice(nx - RADIUS, nx)}
    send_y = {-1: slice(0, SIDE), 0: slice(0, ny), 1: slice(ny - SIDE, ny)}
    land_x = {-1: slice(nx + RADIUS, nx + 2 * RADIUS), 0: slice(RADIUS, RADIUS + nx), 1: slice(0, RADIUS)}
    land_y = {-1: slice(SIDE + ny, 2 * SIDE + ny), 0: slice(SIDE, SIDE + ny), 1: slice(0, SIDE)}

    def halo(i, dx, dy):
        return pltpu.make_async_remote_copy(
            src_ref=spectra.at[send_x[dx], send_y[dy], :],
            dst_ref=ext.at[land_x[dx], land_y[dy], :],
            send_sem=halo_send.at[i],
            recv_sem=halo_recv.at[i],
            device_id={"gx": gx + dx, "gy": gy + dy, "ma": ma},
            device_id_type=MESH,
        )

    barrier = pltpu.get_barrier_semaphore()
    for d in range(1, GROUP):
        for to in (z_peer((ma + d) % GROUP), y_peer((y + d) % GROUP), xc_peer((xc + d) % GROUP)):
            pl.semaphore_signal(barrier, inc=1, device_id=to, device_id_type=MESH)
    for dx, dy in steps:
        @pl.when(exists(dx, dy))
        def _():
            pl.semaphore_signal(
                barrier, inc=1, device_id={"gx": gx + dx, "gy": gy + dy, "ma": ma}, device_id_type=MESH
            )
    near_x = (gx > 0).astype(jnp.int32) + (gx < count_x - 1).astype(jnp.int32)
    near_y = (gy > 0).astype(jnp.int32) + (gy < count_y - 1).astype(jnp.int32)
    pl.semaphore_wait(barrier, 3 * (GROUP - 1) + near_x + near_y + near_x * near_y)

    for i, (dx, dy) in enumerate(steps):
        @pl.when(exists(dx, dy))
        def _():
            halo(i, dx, dy).start()

    def exchange(stage, me, peer_id, source, slots):
        for d in ORDER:
            p = (me + d) % GROUP
            send_one(stage, d, me, p, peer_id, source(p), slots)

    def send_one(stage, d, me, p, peer_id, source, slots):
        pltpu.make_async_remote_copy(
            src_ref=source,
            dst_ref=slots.at[me],
            send_sem=send_sem.at[stage, d - 1],
            recv_sem=recv_sem.at[stage, d - 1],
            device_id=peer_id(p),
            device_id_type=MESH,
        ).start()

    def arrive(stage, me, peer_id, source, slots):
        for d in ORDER[::-1]:
            p = (me + d) % GROUP
            q = (me + GROUP - d) % GROUP
            out = pltpu.make_async_remote_copy(
                src_ref=source(p),
                dst_ref=slots.at[q],
                send_sem=send_sem.at[stage, d - 1],
                recv_sem=recv_sem.at[stage, d - 1],
                device_id=peer_id(p),
                device_id_type=MESH,
            )
            out.wait_recv()
            out.wait_send()

    def total(slots):
        out = slots[0]
        for p in range(1, GROUP):
            out = out + slots[p]
        return out

    zero_x = jnp.zeros((RADIUS, ny + 2 * SIDE, ext.shape[2]), BF16)
    zero_y = jnp.zeros((nx + 2 * RADIUS, SIDE, ext.shape[2]), BF16)

    @pl.when(gx == 0)
    def _():
        ext[0:RADIUS, :, :] = zero_x

    @pl.when(gx == count_x - 1)
    def _():
        ext[nx + RADIUS:nx + 2 * RADIUS, :, :] = zero_x

    @pl.when(gy == 0)
    def _():
        ext[:, 0:SIDE, :] = zero_y

    @pl.when(gy == count_y - 1)
    def _():
        ext[:, SIDE + ny:2 * SIDE + ny, :] = zero_y

    copy_load.wait()
    for x in range(nx):
        load_flat[x // 2, :, 128 * (x % 2):128 * (x % 2) + 128] = load_in[:, x, :]
    full = jnp.zeros((32, 128), F32)
    for i in range(nx // 2):
        part = load_flat[i]
        high, low = split(part)
        load_split[i, 0:32, :] = high
        load_split[i, 32:64, :] = low
        full = full + dot(part, jnp.concatenate([part] * 4, axis=0), NT, HIGH)
    gram_a[xc] = pack_gram(full)
    exchange(0, xc, xc_peer, lambda p: gram_a.at[xc], gram_a)

    hi_taps = weights.astype(ml_dtypes.bfloat16).astype(np.float32)
    lo_taps = (weights - hi_taps).astype(ml_dtypes.bfloat16).astype(np.float32)
    wide = (ny, ny + 2 * SIDE)
    band_hi, band_lo = band(wide, SIDE, hi_taps), band(wide, SIDE, lo_taps)
    band_two = jnp.concatenate([band_hi, band_lo], axis=0).astype(BF16)
    ones = jnp.ones((8, ext.shape[2]), BF16)
    rows[...] = jnp.zeros_like(rows)

    def along_y(x):
        block = ext[x]
        both = dot(band_two, block, NN)
        ysm[x] = both[0:ny] + both[ny:2 * ny]
        rows[pl.ds(x, 1), :] = dot(ones, block, NT)[0:1, :]

    def wait_halo(i):
        dx, dy = steps[i]

        @pl.when(exists(-dx, -dy))
        def _():
            halo(i, dx, dy).wait_recv()

    wait_halo(0)
    wait_halo(1)
    copy_spectra.wait()

    @pl.loop(0, nx // 4)
    def _(i):
        for j in range(4):
            along_y(RADIUS + 4 * i + j)

    for i in range(2, 8):
        wait_halo(i)
    for x in (0, 1, nx + RADIUS, nx + RADIUS + 1):
        along_y(x)

    row_y = dot(rows[...], band_hi + band_lo, NT, HIGH)
    bg_all[ma] = dot(band((nx, rows.shape[0]), RADIUS, weights), row_y, NN, HIGH)
    exchange(1, ma, z_peer, lambda p: bg_all.at[ma], bg_all)

    arrive(0, xc, xc_peer, lambda p: gram_a.at[xc], gram_a)
    gram_b[y] = total(gram_a)
    exchange(2, y, y_peer, lambda p: gram_b.at[y], gram_b)

    w0, w1, w2 = (float(weights[RADIUS + a]) for a in range(3))

    @pl.loop(0, nx // 2)
    def _(i):
        for j in range(2):
            x = 2 * i + j
            smooth[x] = (
                w0 * ysm[x + 2] + w1 * (ysm[x + 1] + ysm[x + 3]) + w2 * (ysm[x] + ysm[x + 4])
            )

    copy_prof.wait()
    arrive(2, y, y_peer, lambda p: gram_b.at[y], gram_b)
    gram = unpack_gram(total(gram_b))
    old_prof = prof_in[...]
    below_prof = dot(gram, jnp.concatenate([old_prof] * 4, axis=0), NN, HIGH) + EPSILON

    arrive(1, ma, z_peer, lambda p: bg_all.at[ma], bg_all)
    pad_t[...] = jnp.zeros_like(pad_t)
    pad_t[0:nx, :] = total(bg_all) * (1.0 / 2048.0)
    back = pad_t[...].T

    acc = jnp.zeros((64, 256), F32)
    acc_lo = jnp.zeros((32, 256), F32)
    for i in range(nx // 2):
        for j in range(2):
            x = 2 * i + j
            value = jnp.maximum(smooth[x] - back[:, x:x + 1], 0.0)
            high, low = split(value)
            clean_hi[i, ny * j:ny * j + ny, :] = high
            clean_lo[i, ny * j:ny * j + ny, :] = low
        acc = acc + dot(load_split[i], clean_hi[i], NN)
        acc_lo = acc_lo + dot(load_split[i, 0:32, :], clean_lo[i], NN)
    numer = acc[0:32] + acc[32:64] + acc_lo

    for p in range(GROUP):
        prof_send[p] = numer[8 * (p // 2):8 * (p // 2) + 8, 128 * (p % 2):128 * (p % 2) + 128]
    exchange(3, xc, xc_peer, lambda p: prof_send.at[p], prof_1)
    prof_1[xc] = prof_send[xc]
    arrive(3, xc, xc_peer, lambda p: prof_send.at[p], prof_1)
    prof_2[y] = total(prof_1)
    exchange(4, y, y_peer, lambda p: prof_2.at[y], prof_2)
    arrive(4, y, y_peer, lambda p: prof_2.at[y], prof_2)
    prof_3[xc] = total(prof_2)
    exchange(5, xc, xc_peer, lambda p: prof_3.at[xc], prof_3)
    arrive(5, xc, xc_peer, lambda p: prof_3.at[xc], prof_3)
    numer_prof = jnp.concatenate(
        [jnp.concatenate([prof_3[2 * b], prof_3[2 * b + 1]], axis=1) for b in range(4)], axis=0
    )
    new_prof = old_prof * numer_prof / below_prof
    prof_new[...] = new_prof
    copy_new = pltpu.make_async_copy(prof_new, out_prof, local_sem.at[3])
    copy_new.start()

    prof_hi, prof_lo = split(new_prof)
    prof_two = jnp.concatenate([prof_hi, prof_lo], axis=0)

    def loading_part(p):
        both = dot(prof_two, clean_hi[p], NT)
        return both[0:32] + both[32:64] + dot(prof_hi, clean_lo[p], NT)

    for d in ORDER:
        p = (ma + d) % GROUP
        part_send[p] = loading_part(p)
        send_one(6, d, ma, p, z_peer, part_send.at[p], part_all)
    gram_c[ma] = pack_gram(dot(new_prof, jnp.concatenate([new_prof] * 4, axis=0), NT, HIGH))
    exchange(7, ma, z_peer, lambda p: gram_c.at[ma], gram_c)
    part_all[ma] = loading_part(ma)

    arrive(7, ma, z_peer, lambda p: gram_c.at[ma], gram_c)
    mine = load_flat[ma]
    below = dot(unpack_gram(total(gram_c)), jnp.concatenate([mine] * 4, axis=0), NN, HIGH) + EPSILON
    arrive(6, ma, z_peer, lambda p: part_send.at[p], part_all)
    new_all[...] = mine * total(part_all) / below

    for d in ORDER:
        p = (ma + d) % GROUP
        send_one(8, d, ma, p, z_peer, new_all, out_load)
    copy_mine = pltpu.make_async_copy(new_all, out_load.at[ma], local_sem.at[4])
    copy_mine.start()
    for i, (dx, dy) in enumerate(steps):
        @pl.when(exists(dx, dy))
        def _():
            halo(i, dx, dy).wait_send()
    copy_new.wait()
    copy_mine.wait()
    arrive(8, ma, z_peer, lambda p: new_all, out_load)


def per_device(spectra, loadings, profiles):
    nx, ny, nm = spectra.shape
    nk = loadings.shape[0]
    wide_x, wide_y = nx + 2 * RADIUS, ny + 2 * SIDE
    anywhere = pl.BlockSpec(memory_space=pl.ANY)
    vmem = pltpu.VMEM
    pieces, new_prof = pl.pallas_call(
        kernel,
        out_shape=(
            jax.ShapeDtypeStruct((GROUP, nk, 2 * ny), F32),
            jax.ShapeDtypeStruct((nk, nm), F32),
        ),
        in_specs=[anywhere] * 3,
        out_specs=(anywhere, anywhere),
        scratch_shapes=[
            vmem((wide_x, wide_y, nm), BF16),
            vmem((nk, nx, ny), F32),
            vmem((nk, nm), F32),
            vmem((wide_x, ny, nm), F32),
            vmem((nx, ny, nm), F32),
            vmem((24, wide_y), F32),
            vmem((GROUP, nk, 2 * ny), F32),
            vmem((GROUP, 2 * nk, 2 * ny), BF16),
            vmem((GROUP, 2 * ny, nm), BF16),
            vmem((GROUP, 2 * ny, nm), BF16),
            vmem((GROUP, nx, ny), F32),
            vmem((GROUP, 8, 128), F32),
            vmem((GROUP, 8, 128), F32),
            vmem((GROUP, 8, 128), F32),
            vmem((GROUP, 8, 128), F32),
            vmem((GROUP, 8, 128), F32),
            vmem((GROUP, 8, 128), F32),
            vmem((nk, nm), F32),
            vmem((GROUP, 8, 128), F32),
            vmem((GROUP, nk, 2 * ny), F32),
            vmem((GROUP, nk, 2 * ny), F32),
            vmem((nk, 2 * ny), F32),
            vmem((128, 128), F32),
            pltpu.SemaphoreType.DMA((5,)),
            pltpu.SemaphoreType.DMA((8,)),
            pltpu.SemaphoreType.DMA((8,)),
            pltpu.SemaphoreType.DMA((9, GROUP - 1)),
            pltpu.SemaphoreType.DMA((9, GROUP - 1)),
        ],
        compiler_params=pltpu.CompilerParams(
            collective_id=0, has_side_effects=True, vmem_limit_bytes=40 * 1024 * 1024
        ),
    )(spectra, loadings, profiles)
    new_load = jnp.transpose(pieces.reshape(GROUP, nk, 2, ny), (1, 0, 2, 3)).reshape(nk, nx, ny)
    return new_load, new_prof


def solution(mesh):
    return jax.shard_map(
        per_device,
        mesh=mesh,
        in_specs=(P("gx", "gy", "ma"), P(None, "gx", "gy"), P(None, "ma")),
        out_specs=(P(None, "gx", "gy"), P(None, "ma")),
        check_vma=False,
    )
```

time: 390 us -> 64.4 us (0.17); the launches traced: 385 us -> 64.2 us
  blocking collectives: 273 us -> 0 us
  waiting for transfers between devices: 63 us -> 0 us
  Pallas kernels: 0 us -> 59.1 us
  starting transfers between devices: 14.6 us -> 0 us
  between operations: 14.2 us -> 0.66 us
  other arithmetic: 12.3 us -> 0 us
  matrix products: 5.39 us -> 0 us
    psum x3 -> x0, blocking collectives: 273 us -> none  [the longest x1 233 us: per_device(): numer_prof, gram_load = lax.psum((numer_part, gram_part), ('gx', 'gy'))]
    pallas_call x0 -> x1, Pallas kernels: none -> 59.1 us  [per_device(): pl.pallas_call(kernel, out_shape=(jax.ShapeDtypeStruct((GROUP, nk, 2 * ny...]
    psum x1 -> x0, waiting for transfers between devices: 58.3 us -> none  [per_device(): numer_load, gram_prof = lax.psum((numer_local, gram_local), 'ma')]
    ppermute x4 -> x0, starting transfers between devices: 14.6 us -> none  [the longest x2 9.24 us: extended(): lax.ppermute(lax.slice_in_dim(block, block.shape[dim] - width, None, axis...]
    dot_general x6 -> x0, matrix products: 5.39 us -> none  [the longest x1 2.77 us: per_device(): numer_local = jnp.einsum('km,xym->kxy', new_prof, cleaned, precision=high)]
    reduce_sum x2 -> x0, other arithmetic: 5.36 us -> none  [the longest x1 4.74 us: per_device(): partial_bg = jnp.sum(smoothed, axis=2)]
    ppermute x4 -> x0, waiting for transfers between devices: 4.74 us -> none  [the longest x2 4.74 us: extended(): lax.ppermute(lax.slice_in_dim(block, 0, width, axis=dim), axis, backward)]
  transfers between devices with their start and end apart: 5 -> 0, of which waited for: 3 -> 0; matrix products, arithmetic and copies ran while one was open for 1% -> 0% of each run, Pallas kernels for 0% -> 0%
where the time goes in v1:
time: 64.4 us; the launch traced here: 64.2 us
  Pallas kernels  59.1 us (92%)
  local copies, waits for them, and re-layouts  4.47 us (7%)
  between operations  0.66 us (1%)
    pallas_call x1, Pallas kernels, per_device(): pl.pallas_call(kernel, out_shape=(jax.ShapeDtypeStruct((GROUP, nk, 2 * ny...  59.1 us
    unnamed x7, local copies, waits for them, and re-layouts  3.54 us

profile of v1, /device:TPU:1, one launch (start us, length us, event | category | flops | bytes accessed | tf_op | source)
XLA Modules:
  0.0 64.2 jit_solution(1955896722875263464)
XLA Ops:
  0.6 0.0 copy-start
  0.6 1.2 %copy-done = bf16[16,128,256]{2,1,0:T(8,128)(2,1)S(1)} copy-done((bf16[16,128,256]{2,1,0:T(8,128)(2,1)S(1)}, bf16[16,128,256]{2,1,0:T(8,128)(2,1)}, u32[]{:S(2)}) %copy-start) | copy-done | bytes 1048600
  1.9 0.0 copy-start.1
  1.9 0.9 %copy-done.1 = f32[32,16,128]{2,1,0:T(8,128)S(1)} copy-done((f32[32,16,128]{2,1,0:T(8,128)S(1)}, f32[32,16,128]{2,1,0:T(8,128)}, u32[]{:S(2)}) %copy-start.1) | copy-done | bytes 262168
  2.8 0.0 copy-start.2
  2.8 0.8 %copy-done.2 = f32[32,256]{1,0:T(8,128)S(1)} copy-done((f32[32,256]{1,0:T(8,128)S(1)}, f32[32,256]{1,0:T(8,128)}, u32[]{:S(2)}) %copy-start.2) | copy-done | bytes 32792
  3.6 59.1 %shard_map.50 = (f32[8,32,256]{2,1,0:T(8,128)S(1)}, f32[32,256]{1,0:T(8,128)S(1)}) custom-call(bf16[16,128,256]{2,1,0:T(8,128)(2,1)S(1)} %copy-done, f32[32,16,128]{2,1,0:T(8,128)S(1)} %copy-done.1, f32[32,256]{1,0:T(8,128)S(1)} %copy-done.2), custom_call_target="tpu_custom_call" | custom-call | tf_op jit(solution)/shard_map/pallas_call | solution.py:354
  62.6 0.1 reshape.10
  62.8 0.8 %copy.5 = f32[32,8,2,128]{3,2,1,0:T(2,128)} copy(f32[32,8,2,128]{3,2,0,1:T(2,128)S(1)} %bitcast.2) | data formatting | bytes 524288 | tf_op jit(solution)/shard_map/transpose | solution.py:396
  63.6 0.6 copy.7
Async XLA Ops:
  0.6 1.2 %copy-start = (bf16[16,128,256]{2,1,0:T(8,128)(2,1)S(1)}, bf16[16,128,256]{2,1,0:T(8,128)(2,1)}, u32[]{:S(2)}) copy-start(bf16[16,128,256]{2,1,0:T(8,128)(2,1)} %spectra.1) | copy-start | bytes 3145732
  1.9 0.9 %copy-start.1 = (f32[32,16,128]{2,1,0:T(8,128)S(1)}, f32[32,16,128]{2,1,0:T(8,128)}, u32[]{:S(2)}) copy-start(f32[32,16,128]{2,1,0:T(8,128)} %loadings.1) | copy-start | bytes 786436
  2.8 0.8 %copy-start.2 = (f32[32,256]{1,0:T(8,128)S(1)}, f32[32,256]{1,0:T(8,128)}, u32[]{:S(2)}) copy-start(f32[32,256]{1,0:T(8,128)} %profiles.1) | copy-start | bytes 98308

commit v2 on v1

v2 whole, which is shorter than its diff:
```python
import jax
import jax.numpy as jnp
import ml_dtypes
import numpy as np
from jax import lax
from jax.experimental import pallas as pl
from jax.experimental.pallas import tpu as pltpu
from jax.sharding import PartitionSpec as P

MESH = pl.DeviceIdType.MESH
F32 = jnp.float32
BF16 = jnp.bfloat16
HIGH = lax.Precision.HIGHEST

RADIUS = 2
SIDE = 16
GROUP = 8
EPSILON = 1e-06
ORDER = (4, 3, 5, 2, 6, 1, 7)

NT = (((1,), (1,)), ((), ()))
NN = (((1,), (0,)), ((), ()))


def taps():
    offsets = np.arange(-RADIUS, RADIUS + 1).astype(np.float32)
    raw = np.exp(-offsets * offsets / np.float32(2.0))
    return (raw / np.sum(raw)).astype(np.float32)


def split(value):
    high = value.astype(BF16)
    return high, (value - high.astype(F32)).astype(BF16)


def dot(a, b, dims, precision=None):
    return lax.dot_general(a, b, dims, precision=precision, preferred_element_type=F32)


def band(shape, shift, weights):
    row = lax.broadcasted_iota(jnp.int32, shape, 0)
    column = lax.broadcasted_iota(jnp.int32, shape, 1)
    at = column - row - shift
    out = jnp.zeros(shape, F32)
    for a in range(-RADIUS, RADIUS + 1):
        out = jnp.where(at == a, float(weights[a + RADIUS]), out)
    return out


def block_mask(b):
    lane = lax.broadcasted_iota(jnp.int32, (8, 128), 1)
    return jnp.logical_and(lane >= 32 * b, lane < 32 * (b + 1))


def pack_gram(full):
    out = jnp.zeros((8, 128), F32)
    for b in range(4):
        out = jnp.where(block_mask(b), full[8 * b:8 * b + 8, :], out)
    return out


def unpack_gram(packed):
    return jnp.concatenate([jnp.where(block_mask(b), packed, 0.0) for b in range(4)], axis=0)


def kernel(
    spectra, loadings, profiles, out_load, out_prof,
    ext, load_in, prof_in, ysm, smooth, rows, load_flat, load_split, clean_hi, clean_lo,
    bg_all, gram_a, gram_b, prof_send, prof_1, prof_2, prof_3, prof_new,
    gram_c, part_send, part_all, below_all, new_all, pad_t,
    local_sem, halo_send, halo_recv, send_sem, recv_sem, part_recv,
):
    nx, ny, nm = spectra.shape
    nk = loadings.shape[0]
    own = nk // GROUP
    gx, gy, ma = lax.axis_index("gx"), lax.axis_index("gy"), lax.axis_index("ma")
    count_x, count_y = lax.axis_size("gx"), lax.axis_size("gy")
    half, y = gy // GROUP, gy % GROUP
    xc = gx * 2 + half
    weights = taps()

    def z_peer(p):
        return {"gx": gx, "gy": gy, "ma": p}

    def y_peer(p):
        return {"gx": gx, "gy": half * GROUP + p, "ma": ma}

    def xc_peer(p):
        return {"gx": p // 2, "gy": (p % 2) * GROUP + y, "ma": ma}

    copy_spectra = pltpu.make_async_copy(
        spectra, ext.at[RADIUS:RADIUS + nx, SIDE:SIDE + ny, :], local_sem.at[0]
    )
    copy_load = pltpu.make_async_copy(loadings, load_in, local_sem.at[1])
    copy_prof = pltpu.make_async_copy(profiles, prof_in, local_sem.at[2])

    has = {
        ("x", -1): gx > 0, ("x", 0): None, ("x", 1): gx < count_x - 1,
        ("y", -1): gy > 0, ("y", 0): None, ("y", 1): gy < count_y - 1,
    }
    steps = [(-1, 0), (1, 0), (0, -1), (0, 1), (-1, -1), (-1, 1), (1, -1), (1, 1)]

    def exists(dx, dy):
        a, b = has[("x", dx)], has[("y", dy)]
        if a is None:
            return b
        if b is None:
            return a
        return jnp.logical_and(a, b)

    send_x = {-1: slice(0, RADIUS), 0: slice(0, nx), 1: slice(nx - RADIUS, nx)}
    send_y = {-1: slice(0, SIDE), 0: slice(0, ny), 1: slice(ny - SIDE, ny)}
    land_x = {-1: slice(nx + RADIUS, nx + 2 * RADIUS), 0: slice(RADIUS, RADIUS + nx), 1: slice(0, RADIUS)}
    land_y = {-1: slice(SIDE + ny, 2 * SIDE + ny), 0: slice(SIDE, SIDE + ny), 1: slice(0, SIDE)}

    def halo(i, dx, dy):
        return pltpu.make_async_remote_copy(
            src_ref=spectra.at[send_x[dx], send_y[dy], :],
            dst_ref=ext.at[land_x[dx], land_y[dy], :],
            send_sem=halo_send.at[i],
            recv_sem=halo_recv.at[i],
            device_id={"gx": gx + dx, "gy": gy + dy, "ma": ma},
            device_id_type=MESH,
        )

    barrier = pltpu.get_barrier_semaphore()
    for dx, dy in steps:
        @pl.when(exists(dx, dy))
        def _():
            pl.semaphore_signal(
                barrier, inc=1, device_id={"gx": gx + dx, "gy": gy + dy, "ma": ma}, device_id_type=MESH
            )
    for d in ORDER:
        for to in (z_peer((ma + d) % GROUP), y_peer((y + d) % GROUP), xc_peer((xc + d) % GROUP)):
            pl.semaphore_signal(barrier, inc=1, device_id=to, device_id_type=MESH)
    copy_spectra.start()
    copy_load.start()
    copy_prof.start()
    near_x = (gx > 0).astype(jnp.int32) + (gx < count_x - 1).astype(jnp.int32)
    near_y = (gy > 0).astype(jnp.int32) + (gy < count_y - 1).astype(jnp.int32)
    pl.semaphore_wait(barrier, 3 * (GROUP - 1) + near_x + near_y + near_x * near_y)

    for i, (dx, dy) in enumerate(steps):
        @pl.when(exists(dx, dy))
        def _():
            halo(i, dx, dy).start()

    def copy(stage, source, target, device, recv=None):
        return pltpu.make_async_remote_copy(
            src_ref=source,
            dst_ref=target,
            send_sem=send_sem.at[stage],
            recv_sem=recv_sem.at[stage] if recv is None else recv,
            device_id=device,
            device_id_type=MESH,
        )

    def exchange(stage, me, peer_id, source, slots):
        for d in ORDER:
            p = (me + d) % GROUP
            copy(stage, source(p), slots.at[me], peer_id(p)).start()

    def arrive(stage, me, peer_id, slots):
        whole = slots.at[0:GROUP - 1]
        copy(stage, whole, whole, peer_id((me + 1) % GROUP)).wait_recv()

    def sent(stage, me, peer_id, slots):
        whole = slots.at[0:GROUP - 1]
        copy(stage, whole, whole, peer_id((me + 1) % GROUP)).wait_send()

    def total(slots):
        out = slots[0]
        for p in range(1, GROUP):
            out = out + slots[p]
        return out

    zero_x = jnp.zeros((RADIUS, ny + 2 * SIDE, nm), BF16)
    zero_y = jnp.zeros((nx + 2 * RADIUS, SIDE, nm), BF16)

    @pl.when(gx == 0)
    def _():
        ext[0:RADIUS, :, :] = zero_x

    @pl.when(gx == count_x - 1)
    def _():
        ext[nx + RADIUS:nx + 2 * RADIUS, :, :] = zero_x

    @pl.when(gy == 0)
    def _():
        ext[:, 0:SIDE, :] = zero_y

    @pl.when(gy == count_y - 1)
    def _():
        ext[:, SIDE + ny:2 * SIDE + ny, :] = zero_y

    copy_load.wait()
    for x in range(nx):
        load_flat[x // 2, :, 128 * (x % 2):128 * (x % 2) + 128] = load_in[:, x, :]
    full = jnp.zeros((32, 128), F32)
    for i in range(nx // 2):
        part = load_flat[i]
        high, low = split(part)
        load_split[i, 0:32, :] = high
        load_split[i, 32:64, :] = low
        full = full + dot(part, jnp.concatenate([part] * 4, axis=0), NT, HIGH)
    gram_a[xc] = pack_gram(full)
    exchange(0, xc, xc_peer, lambda p: gram_a.at[xc], gram_a)

    ones = jnp.ones((8, nm), BF16)
    rows[...] = jnp.zeros_like(rows)

    def sum_bins(x):
        rows[x:x + 1, :] = dot(ones, ext[x], NT)[0:1, :]

    def wait_halo(i):
        dx, dy = steps[i]

        @pl.when(exists(-dx, -dy))
        def _():
            halo(i, dx, dy).wait_recv()

    copy_spectra.wait()
    wait_halo(2)
    wait_halo(3)
    for x in range(RADIUS, nx + RADIUS):
        sum_bins(x)
    for i in (0, 1, 4, 5, 6, 7):
        wait_halo(i)
    for x in (0, 1, nx + RADIUS, nx + RADIUS + 1):
        sum_bins(x)

    hi_taps = weights.astype(ml_dtypes.bfloat16).astype(np.float32)
    lo_taps = (weights - hi_taps).astype(ml_dtypes.bfloat16).astype(np.float32)
    wide = (ny, ny + 2 * SIDE)
    band_hi, band_lo = band(wide, SIDE, hi_taps), band(wide, SIDE, lo_taps)
    w0, w1, w2 = (float(weights[RADIUS + a]) for a in range(3))
    row_x = (
        w0 * rows[2:nx + 2, :] + w1 * (rows[1:nx + 1, :] + rows[3:nx + 3, :])
        + w2 * (rows[0:nx, :] + rows[4:nx + 4, :])
    )
    bg_all[ma] = dot(row_x, band_hi + band_lo, NT, HIGH)
    exchange(1, ma, z_peer, lambda p: bg_all.at[ma], bg_all)

    arrive(0, xc, xc_peer, gram_a)
    gram_b[y] = total(gram_a)
    exchange(2, y, y_peer, lambda p: gram_b.at[y], gram_b)
    band_two = jnp.concatenate([band_hi, band_lo], axis=0).astype(BF16)

    @pl.loop(0, (nx + 2 * RADIUS) // 4)
    def _(i):
        for j in range(4):
            x = 4 * i + j
            both = dot(band_two, ext[x], NN)
            ysm[x] = both[0:ny] + both[ny:2 * ny]

    @pl.loop(0, nx // 2)
    def _(i):
        for j in range(2):
            x = 2 * i + j
            smooth[x] = (
                w0 * ysm[x + 2] + w1 * (ysm[x + 1] + ysm[x + 3]) + w2 * (ysm[x] + ysm[x + 4])
            )

    copy_prof.wait()
    arrive(2, y, y_peer, gram_b)
    gram = unpack_gram(total(gram_b))
    old_prof = prof_in[...]
    below_prof = dot(gram, jnp.concatenate([old_prof] * 4, axis=0), NN, HIGH) + EPSILON

    arrive(1, ma, z_peer, bg_all)
    pad_t[0:nx, :] = total(bg_all) * (1.0 / 2048.0)
    back = pad_t[...].T

    acc = jnp.zeros((64, 256), F32)
    acc_lo = jnp.zeros((32, 256), F32)
    for i in range(nx // 2):
        for j in range(2):
            x = 2 * i + j
            value = jnp.maximum(smooth[x] - back[:, x:x + 1], 0.0)
            high, low = split(value)
            clean_hi[i, ny * j:ny * j + ny, :] = high
            clean_lo[i, ny * j:ny * j + ny, :] = low
        acc = acc + dot(load_split[i], clean_hi[i], NN)
        acc_lo = acc_lo + dot(load_split[i, 0:32, :], clean_lo[i], NN)
    numer = acc[0:32] + acc[32:64] + acc_lo

    for p in range(GROUP):
        prof_send[p] = numer[8 * (p // 2):8 * (p // 2) + 8, 128 * (p % 2):128 * (p % 2) + 128]
    exchange(3, xc, xc_peer, lambda p: prof_send.at[p], prof_1)
    prof_1[xc] = prof_send[xc]
    arrive(3, xc, xc_peer, prof_1)
    prof_2[y] = total(prof_1)
    exchange(4, y, y_peer, lambda p: prof_2.at[y], prof_2)
    arrive(4, y, y_peer, prof_2)
    prof_3[xc] = total(prof_2)
    exchange(5, xc, xc_peer, lambda p: prof_3.at[xc], prof_3)
    arrive(5, xc, xc_peer, prof_3)
    numer_prof = jnp.concatenate(
        [jnp.concatenate([prof_3[2 * b], prof_3[2 * b + 1]], axis=1) for b in range(4)], axis=0
    )
    new_prof = old_prof * numer_prof / below_prof

    prof_hi, prof_lo = split(new_prof)
    prof_two = jnp.concatenate([prof_hi, prof_lo], axis=0)
    for i in range(nx // 2):
        both = dot(prof_two, clean_hi[i], NT)
        part = both[0:32] + both[32:64] + dot(prof_hi, clean_lo[i], NT)
        part_send[:, 2 * i, :] = part[:, 0:ny]
        part_send[:, 2 * i + 1, :] = part[:, ny:2 * ny]
    for c in range(own):
        for d in ORDER:
            p = (ma + d) % GROUP
            copy(6, part_send.at[own * p + c], part_all.at[c, d - 1], z_peer(p), part_recv.at[c]).start()
        if c == 0:
            gram_c[ma] = pack_gram(dot(new_prof, jnp.concatenate([new_prof] * 4, axis=0), NT, HIGH))
            exchange(7, ma, z_peer, lambda p: gram_c.at[ma], gram_c)
    prof_new[...] = new_prof
    copy_new = pltpu.make_async_copy(prof_new, out_prof, local_sem.at[3])
    copy_new.start()

    arrive(7, ma, z_peer, gram_c)
    lane = lax.broadcasted_iota(jnp.int32, (8, 128), 1)
    block = ma // 2
    mask = jnp.logical_and(lane >= 32 * block, lane < 32 * block + 32)
    gram_rows = jnp.where(mask, total(gram_c), 0.0)
    for i in range(nx // 2):
        below = dot(gram_rows, jnp.concatenate([load_flat[i]] * 4, axis=0), NN, HIGH) + EPSILON
        below_all[:, 2 * i, :] = below[:, 0:ny]
        below_all[:, 2 * i + 1, :] = below[:, ny:2 * ny]

    for c in range(own):
        whole = part_all.at[c]
        copy(6, whole, whole, z_peer((ma + 1) % GROUP), part_recv.at[c]).wait_recv()
        k = own * ma + c
        value = part_send[k]
        for d in range(GROUP - 1):
            value = value + part_all[c, d]
        new_all[c] = load_in[k] * value / below_all[own * (ma % 2) + c]
        for p in range(GROUP):
            @pl.when(ma != p)
            def _():
                copy(8, new_all.at[c], out_load.at[k], z_peer(p)).start()
    copy_mine = pltpu.make_async_copy(new_all, out_load.at[pl.ds(own * ma, own)], local_sem.at[4])
    copy_mine.start()

    for i, (dx, dy) in enumerate(steps):
        @pl.when(exists(dx, dy))
        def _():
            halo(i, dx, dy).wait_send()
    sent(0, xc, xc_peer, gram_a)
    sent(1, ma, z_peer, bg_all)
    sent(2, y, y_peer, gram_b)
    sent(3, xc, xc_peer, prof_1)
    sent(4, y, y_peer, prof_2)
    sent(5, xc, xc_peer, prof_3)
    sent(7, ma, z_peer, gram_c)
    peer = z_peer((ma + 1) % GROUP)
    copy(6, part_all, part_all, peer).wait_send()
    copy_new.wait()
    copy_mine.wait()
    most = out_load.at[0:nk - own]
    copy(8, most, most, peer).wait_send()
    copy(8, most, most, peer).wait_recv()


def per_device(spectra, loadings, profiles):
    nx, ny, nm = spectra.shape
    nk = loadings.shape[0]
    own = nk // GROUP
    wide_x, wide_y = nx + 2 * RADIUS, ny + 2 * SIDE
    anywhere = pl.BlockSpec(memory_space=pl.ANY)
    vmem = pltpu.VMEM
    return pl.pallas_call(
        kernel,
        out_shape=(
            jax.ShapeDtypeStruct((nk, nx, ny), F32),
            jax.ShapeDtypeStruct((nk, nm), F32),
        ),
        in_specs=[anywhere] * 3,
        out_specs=(anywhere, anywhere),
        scratch_shapes=[
            vmem((wide_x, wide_y, nm), BF16),
            vmem((nk, nx, ny), F32),
            vmem((nk, nm), F32),
            vmem((wide_x, ny, nm), F32),
            vmem((nx, ny, nm), F32),
            vmem((24, wide_y), F32),
            vmem((nx // 2, nk, 2 * ny), F32),
            vmem((nx // 2, 2 * nk, 2 * ny), BF16),
            vmem((nx // 2, 2 * ny, nm), BF16),
            vmem((nx // 2, 2 * ny, nm), BF16),
            vmem((GROUP, nx, ny), F32),
            vmem((GROUP, 8, 128), F32),
            vmem((GROUP, 8, 128), F32),
            vmem((GROUP, 8, 128), F32),
            vmem((GROUP, 8, 128), F32),
            vmem((GROUP, 8, 128), F32),
            vmem((GROUP, 8, 128), F32),
            vmem((nk, nm), F32),
            vmem((GROUP, 8, 128), F32),
            vmem((nk, nx, ny), F32),
            vmem((own, GROUP - 1, nx, ny), F32),
            vmem((8, nx, ny), F32),
            vmem((own, nx, ny), F32),
            vmem((128, 128), F32),
            pltpu.SemaphoreType.DMA((5,)),
            pltpu.SemaphoreType.DMA((8,)),
            pltpu.SemaphoreType.DMA((8,)),
            pltpu.SemaphoreType.DMA((9,)),
            pltpu.SemaphoreType.DMA((9,)),
            pltpu.SemaphoreType.DMA((own,)),
        ],
        compiler_params=pltpu.CompilerParams(
            collective_id=0, has_side_effects=True, vmem_limit_bytes=60 * 1024 * 1024
        ),
    )(spectra, loadings, profiles)


def solution(mesh):
    return jax.shard_map(
        per_device,
        mesh=mesh,
        in_specs=(P("gx", "gy", "ma"), P(None, "gx", "gy"), P(None, "ma")),
        out_specs=(P(None, "gx", "gy"), P(None, "ma")),
        check_vma=False,
    )
```

time: 64.4 us -> 58.7 us (0.911)
  Pallas kernels: 59.1 us -> 55.6 us
  local copies, waits for them, and re-layouts: 4.47 us -> 2.29 us
    pallas_call x1, Pallas kernels: 59.1 us -> 55.6 us  [per_device(): pl.pallas_call(kernel, out_shape=(jax.ShapeDtypeStruct((nk, nx, ny), F32)...]
    unnamed x7 -> x4, local copies, waits for them, and re-layouts: 3.54 us -> 2.29 us
    transpose x1 -> x0, local copies, waits for them, and re-layouts: 0.79 us -> none  [per_device(): jnp.transpose(pieces.reshape(GROUP, nk, 2, ny), (1, 0, 2, 3))]
where the time goes in v2:
time: 58.7 us; the launch traced here: 58.5 us
  Pallas kernels  55.6 us (95%)
  local copies, waits for them, and re-layouts  2.29 us (4%)
  between operations  0.65 us (1%)
    pallas_call x1, Pallas kernels, per_device(): pl.pallas_call(kernel, out_shape=(jax.ShapeDtypeStruct((nk, nx, ny), F32)...  55.6 us
    unnamed x4, local copies, waits for them, and re-layouts  2.29 us

profile of v2, /device:TPU:1, one launch (start us, length us, event | category | flops | bytes accessed | tf_op | source)
XLA Modules:
  0.0 58.5 jit_solution(14098131925807921986)
XLA Ops:
  0.6 55.6 %shard_map.50 = (f32[32,16,128]{2,1,0:T(8,128)}, f32[32,256]{1,0:T(8,128)}) custom-call(bf16[16,128,256]{2,1,0:T(8,128)(2,1)} %spectra.1, f32[32,16,128]{2,1,0:T(8,128)} %loadings.1, f32[32,256]{1,0:T(8,128)} %profiles.1), custom_call_target="tpu_custom_call" | custom-call | tf_op jit(solution)/shard_map/pallas_call | solution.py:373
  56.2 0.0 copy-start
  56.2 1.7 %copy.7 = f32[32,16,128]{2,1,0:T(8,128)} copy(f32[32,16,128]{2,1,0:T(8,128)} %get-tuple-element.4) | data formatting | bytes 524288
  57.9 0.0 copy-done
  57.9 0.6 %copy.8 = f32[32,256]{1,0:T(8,128)} copy(f32[32,256]{1,0:T(8,128)S(1)} %copy-done) | data formatting | bytes 65536
Async XLA Ops:
  56.2 1.7 %copy-start = (f32[32,256]{1,0:T(8,128)S(1)}, f32[32,256]{1,0:T(8,128)}, u32[]{:S(2)}) copy-start(f32[32,256]{1,0:T(8,128)} %get-tuple-element.5) | copy-start | bytes 98308

commit v3 on v2

--- a/solution.py
+++ b/solution.py
@@ -68,7 +68,7 @@
     ext, load_in, prof_in, ysm, smooth, rows, load_flat, load_split, clean_hi, clean_lo,
     bg_all, gram_a, gram_b, prof_send, prof_1, prof_2, prof_3, prof_new,
     gram_c, part_send, part_all, below_all, new_all, pad_t,
-    local_sem, halo_send, halo_recv, send_sem, recv_sem, part_recv,
+    sums_own, sums_in, edge_own, edge_in, local_sem, sums_send, sums_recv, halo_send, halo_recv, send_sem, recv_sem, part_recv,
 ):
     nx, ny, nm = spectra.shape
     nk = loadings.shape[0]
@@ -108,15 +108,22 @@
             return a
         return jnp.logical_and(a, b)
 
-    send_x = {-1: slice(0, RADIUS), 0: slice(0, nx), 1: slice(nx - RADIUS, nx)}
-    send_y = {-1: slice(0, SIDE), 0: slice(0, ny), 1: slice(ny - SIDE, ny)}
-    land_x = {-1: slice(nx + RADIUS, nx + 2 * RADIUS), 0: slice(RADIUS, RADIUS + nx), 1: slice(0, RADIUS)}
-    land_y = {-1: slice(SIDE + ny, 2 * SIDE + ny), 0: slice(SIDE, SIDE + ny), 1: slice(0, SIDE)}
+    rows_out = {-1: slice(0, 16), 0: slice(0, 2 * nx), 1: slice(2 * nx - 16, 2 * nx)}
+    rows_land = {-1: slice(16 + 2 * nx, 32 + 2 * nx), 0: slice(16, 16 + 2 * nx), 1: slice(0, 16)}
+    middle = slice(SIDE, SIDE + ny)
+
+    def halo_refs(dx, dy):
+        if dy == 0:
+            first, land = (RADIUS, nx + RADIUS) if dx < 0 else (nx, 0)
+            return ext.at[first:first + RADIUS, middle, :], ext.at[land:land + RADIUS, middle, :]
+        side = (dy + 1) // 2
+        return edge_own.at[side, rows_out[dx], :], edge_in.at[1 - side, rows_land[dx], :]
 
     def halo(i, dx, dy):
+        source, target = halo_refs(dx, dy)
         return pltpu.make_async_remote_copy(
-            src_ref=spectra.at[send_x[dx], send_y[dy], :],
-            dst_ref=ext.at[land_x[dx], land_y[dy], :],
+            src_ref=source,
+            dst_ref=target,
             send_sem=halo_send.at[i],
             recv_sem=halo_recv.at[i],
             device_id={"gx": gx + dx, "gy": gy + dy, "ma": ma},
@@ -136,14 +143,37 @@
     copy_spectra.start()
     copy_load.start()
     copy_prof.start()
+
+    copy_spectra.wait()
+    ones = jnp.ones((8, nm), BF16)
+    for x in range(nx):
+        sums_own[x:x + 1, :] = dot(ones, ext[RADIUS + x, SIDE:SIDE + ny, :], NT)[0:1, :]
+    at = lax.broadcasted_iota(jnp.int32, (2 * nx, 16 * nx), 0)
+    column = lax.broadcasted_iota(jnp.int32, (2 * nx, 16 * nx), 1)
+    for side, first in ((0, SIDE), (1, SIDE + ny - 16)):
+        tile = ext[RADIUS:RADIUS + nx, first:first + 16, :].reshape(16 * nx, nm)
+        pick = column == 16 * (at >> 1) + (at & 1) + side * (16 - RADIUS)
+        edge_own[side] = dot(jnp.where(pick, 1.0, 0.0).astype(BF16), tile, NN).astype(BF16)
+
     near_x = (gx > 0).astype(jnp.int32) + (gx < count_x - 1).astype(jnp.int32)
     near_y = (gy > 0).astype(jnp.int32) + (gy < count_y - 1).astype(jnp.int32)
     pl.semaphore_wait(barrier, 3 * (GROUP - 1) + near_x + near_y + near_x * near_y)
 
-    for i, (dx, dy) in enumerate(steps):
-        @pl.when(exists(dx, dy))
-        def _():
-            halo(i, dx, dy).start()
+    def sums(i, dx, dy):
+        return pltpu.make_async_remote_copy(
+            src_ref=sums_own,
+            dst_ref=sums_in.at[i],
+            send_sem=sums_send.at[i],
+            recv_sem=sums_recv.at[i],
+            device_id={"gx": gx + dx, "gy": gy + dy, "ma": ma},
+            device_id_type=MESH,
+        )
+
+    for make in (sums, halo):
+        for i, (dx, dy) in enumerate(steps):
+            @pl.when(exists(dx, dy))
+            def _():
+                make(i, dx, dy).start()
 
     def copy(stage, source, target, device, recv=None):
         return pltpu.make_async_remote_copy(
@@ -174,24 +204,11 @@
             out = out + slots[p]
         return out
 
-    zero_x = jnp.zeros((RADIUS, ny + 2 * SIDE, nm), BF16)
-    zero_y = jnp.zeros((nx + 2 * RADIUS, SIDE, nm), BF16)
-
-    @pl.when(gx == 0)
-    def _():
-        ext[0:RADIUS, :, :] = zero_x
-
-    @pl.when(gx == count_x - 1)
-    def _():
-        ext[nx + RADIUS:nx + 2 * RADIUS, :, :] = zero_x
-
-    @pl.when(gy == 0)
-    def _():
-        ext[:, 0:SIDE, :] = zero_y
-
-    @pl.when(gy == count_y - 1)
-    def _():
-        ext[:, SIDE + ny:2 * SIDE + ny, :] = zero_y
+    for dx, dy in steps:
+        @pl.when(jnp.logical_not(exists(-dx, -dy)))
+        def _():
+            unused, target = halo_refs(dx, dy)
+            target[...] = jnp.zeros(target.shape, BF16)
 
     copy_load.wait()
     for x in range(nx):
@@ -206,45 +223,54 @@
     gram_a[xc] = pack_gram(full)
     exchange(0, xc, xc_peer, lambda p: gram_a.at[xc], gram_a)
 
-    ones = jnp.ones((8, nm), BF16)
-    rows[...] = jnp.zeros_like(rows)
-
-    def sum_bins(x):
-        rows[x:x + 1, :] = dot(ones, ext[x], NT)[0:1, :]
-
-    def wait_halo(i):
-        dx, dy = steps[i]
-
-        @pl.when(exists(-dx, -dy))
-        def _():
-            halo(i, dx, dy).wait_recv()
-
-    copy_spectra.wait()
-    wait_halo(2)
-    wait_halo(3)
-    for x in range(RADIUS, nx + RADIUS):
-        sum_bins(x)
-    for i in (0, 1, 4, 5, 6, 7):
-        wait_halo(i)
-    for x in (0, 1, nx + RADIUS, nx + RADIUS + 1):
-        sum_bins(x)
+    for i, (dx, dy) in enumerate(steps):
+        there = exists(-dx, -dy)
+
+        @pl.when(there)
+        def _():
+            sums(i, dx, dy).wait_recv()
+
+        @pl.when(jnp.logical_not(there))
+        def _():
+            sums_in[i] = jnp.zeros_like(sums_own)
+    for side in (-1, 0, 1):
+        columns = slice(ny * (side + 1), ny * (side + 2))
+        low, high = steps.index((1, -side)), steps.index((-1, -side))
+        rows[0:RADIUS, columns] = sums_in[low, nx - RADIUS:nx, :]
+        rows[RADIUS:nx + RADIUS, columns] = sums_own[...] if side == 0 else sums_in[steps.index((0, -side))]
+        rows[nx + RADIUS:nx + 2 * RADIUS, columns] = sums_in[high, 0:RADIUS, :]
 
     hi_taps = weights.astype(ml_dtypes.bfloat16).astype(np.float32)
     lo_taps = (weights - hi_taps).astype(ml_dtypes.bfloat16).astype(np.float32)
     wide = (ny, ny + 2 * SIDE)
-    band_hi, band_lo = band(wide, SIDE, hi_taps), band(wide, SIDE, lo_taps)
+    both_taps = hi_taps + lo_taps
     w0, w1, w2 = (float(weights[RADIUS + a]) for a in range(3))
     row_x = (
         w0 * rows[2:nx + 2, :] + w1 * (rows[1:nx + 1, :] + rows[3:nx + 3, :])
         + w2 * (rows[0:nx, :] + rows[4:nx + 4, :])
     )
-    bg_all[ma] = dot(row_x, band_hi + band_lo, NT, HIGH)
+    bg_all[ma] = dot(row_x, band((ny, 3 * ny), ny, both_taps), NT, HIGH)
     exchange(1, ma, z_peer, lambda p: bg_all.at[ma], bg_all)
 
     arrive(0, xc, xc_peer, gram_a)
     gram_b[y] = total(gram_a)
     exchange(2, y, y_peer, lambda p: gram_b.at[y], gram_b)
-    band_two = jnp.concatenate([band_hi, band_lo], axis=0).astype(BF16)
+    band_two = jnp.concatenate(
+        [band(wide, SIDE, hi_taps), band(wide, SIDE, lo_taps)], axis=0
+    ).astype(BF16)
+    for i, (dx, dy) in enumerate(steps):
+        @pl.when(exists(-dx, -dy))
+        def _():
+            halo(i, dx, dy).wait_recv()
+    at = lax.broadcasted_iota(jnp.int32, (16 * (nx + 2 * RADIUS), edge_in.shape[1]), 0)
+    column = lax.broadcasted_iota(jnp.int32, (16 * (nx + 2 * RADIUS), edge_in.shape[1]), 1)
+    for side, first in ((0, SIDE - 16), (1, SIDE + ny)):
+        inside = (at & 15) - (16 - RADIUS) * (1 - side)
+        pick = jnp.logical_and(
+            column == 12 + 2 * (at >> 4) + inside, jnp.logical_and(inside >= 0, inside < RADIUS)
+        )
+        spread = dot(jnp.where(pick, 1.0, 0.0).astype(BF16), edge_in[side], NN).astype(BF16)
+        ext[:, first:first + 16, :] = spread.reshape(nx + 2 * RADIUS, 16, nm)
 
     @pl.loop(0, (nx + 2 * RADIUS) // 4)
     def _(i):
@@ -347,6 +373,7 @@
         @pl.when(exists(dx, dy))
         def _():
             halo(i, dx, dy).wait_send()
+            sums(i, dx, dy).wait_send()
     sent(0, xc, xc_peer, gram_a)
     sent(1, ma, z_peer, bg_all)
     sent(2, y, y_peer, gram_b)
@@ -363,6 +390,14 @@
     copy(8, most, most, peer).wait_recv()
 
 
+def finish(load, prof, out_load, out_prof, sem):
+    copies = [pltpu.make_async_copy(load, out_load, sem.at[0]), pltpu.make_async_copy(prof, out_prof, sem.at[1])]
+    for c in copies:
+        c.start()
+    for c in copies:
+        c.wait()
+
+
 def per_device(spectra, loadings, profiles):
     nx, ny, nm = spectra.shape
     nk = loadings.shape[0]
@@ -370,11 +405,11 @@
     wide_x, wide_y = nx + 2 * RADIUS, ny + 2 * SIDE
     anywhere = pl.BlockSpec(memory_space=pl.ANY)
     vmem = pltpu.VMEM
-    return pl.pallas_call(
+    held_load, held_prof = pl.pallas_call(
         kernel,
         out_shape=(
-            jax.ShapeDtypeStruct((nk, nx, ny), F32),
-            jax.ShapeDtypeStruct((nk, nm), F32),
+            pltpu.VMEM((nk, nx, ny), F32),
+            pltpu.VMEM((nk, nm), F32),
         ),
         in_specs=[anywhere] * 3,
         out_specs=(anywhere, anywhere),
@@ -384,7 +419,7 @@
             vmem((nk, nm), F32),
             vmem((wide_x, ny, nm), F32),
             vmem((nx, ny, nm), F32),
-            vmem((24, wide_y), F32),
+            vmem((24, 3 * ny), F32),
             vmem((nx // 2, nk, 2 * ny), F32),
             vmem((nx // 2, 2 * nk, 2 * ny), BF16),
             vmem((nx // 2, 2 * ny, nm), BF16),
@@ -403,7 +438,13 @@
             vmem((8, nx, ny), F32),
             vmem((own, nx, ny), F32),
             vmem((128, 128), F32),
+            vmem((nx, ny), F32),
+            vmem((8, nx, ny), F32),
+            vmem((2, 2 * nx, nm), BF16),
+            vmem((2, 2 * nx + 32, nm), BF16),
             pltpu.SemaphoreType.DMA((5,)),
+            pltpu.SemaphoreType.DMA((8,)),
+            pltpu.SemaphoreType.DMA((8,)),
             pltpu.SemaphoreType.DMA((8,)),
             pltpu.SemaphoreType.DMA((8,)),
             pltpu.SemaphoreType.DMA((9,)),
@@ -414,6 +455,16 @@
             collective_id=0, has_side_effects=True, vmem_limit_bytes=60 * 1024 * 1024
         ),
     )(spectra, loadings, profiles)
+    return pl.pallas_call(
+        finish,
+        out_shape=(
+            jax.ShapeDtypeStruct((nk, nx, ny), F32),
+            jax.ShapeDtypeStruct((nk, nm), F32),
+        ),
+        in_specs=[anywhere] * 2,
+        out_specs=(anywhere, anywhere),
+        scratch_shapes=[pltpu.SemaphoreType.DMA((2,))],
+    )(*(pltpu.with_memory_space_constraint(a, pltpu.VMEM) for a in (held_load, held_prof)))
 
 
 def solution(mesh):

time: 58.7 us -> 55.6 us (0.947)
  local copies, waits for them, and re-layouts: 2.29 us -> 0 us
  Pallas kernels: 55.6 us -> 54.8 us
    unnamed x4 -> x0, local copies, waits for them, and re-layouts: 2.29 us -> none
    pallas_call x1 -> x2, Pallas kernels: 55.6 us -> 54.8 us  [the longest x1 54.1 us: per_device(): pl.pallas_call(kernel, out_shape=(pltpu.VMEM((nk, nx, ny), F32), pltpu.VM...]
where the time goes in v3:
time: 55.6 us; the launch traced here: 55.4 us
  Pallas kernels  54.8 us (99%)
  between operations  0.64 us (1%)
    pallas_call x1, Pallas kernels, per_device(): pl.pallas_call(kernel, out_shape=(pltpu.VMEM((nk, nx, ny), F32), pltpu.VM...  54.1 us

profile of v3, /device:TPU:1, one launch (start us, length us, event | category | flops | bytes accessed | tf_op | source)
XLA Modules:
  0.0 55.4 jit_solution(1254979597794653819)
XLA Ops:
  0.6 54.1 %shard_map.50 = (f32[32,16,128]{2,1,0:T(8,128)S(1)}, f32[32,256]{1,0:T(8,128)S(1)}) custom-call(bf16[16,128,256]{2,1,0:T(8,128)(2,1)} %spectra.1, f32[32,16,128]{2,1,0:T(8,128)} %loadings.1, f32[32,256]{1,0:T(8,128)} %profiles.1), custom_call_target="tpu_custom_call" | custom-call | tf_op jit(solution)/shard_map/pallas_call | solution.py:408
  54.7 0.7 %shard_map.51 = (f32[32,16,128]{2,1,0:T(8,128)}, f32[32,256]{1,0:T(8,128)}) custom-call(f32[32,16,128]{2,1,0:T(8,128)S(1)} %get-tuple-element.4.load, f32[32,256]{1,0:T(8,128)S(1)} %get-tuple-element.5.prof), custom_call_target="tpu_custom_call" | custom-call | tf_op jit(solution)/shard_map/pallas_call | solution.py:458

commit v4 on v3

--- a/solution.py
+++ b/solution.py
@@ -16,6 +16,7 @@
 SIDE = 16
 GROUP = 8
 EPSILON = 1e-06
+CHUNKS = 2
 ORDER = (4, 3, 5, 2, 6, 1, 7)
 
 NT = (((1,), (1,)), ((), ()))
@@ -72,6 +73,7 @@
 ):
     nx, ny, nm = spectra.shape
     nk = loadings.shape[0]
+    size = nk // GROUP // CHUNKS
     own = nk // GROUP
     gx, gy, ma = lax.axis_index("gx"), lax.axis_index("gy"), lax.axis_index("ma")
     count_x, count_y = lax.axis_size("gx"), lax.axis_size("gy")
@@ -93,6 +95,9 @@
     )
     copy_load = pltpu.make_async_copy(loadings, load_in, local_sem.at[1])
     copy_prof = pltpu.make_async_copy(profiles, prof_in, local_sem.at[2])
+    copy_spectra.start()
+    copy_load.start()
+    copy_prof.start()
 
     has = {
         ("x", -1): gx > 0, ("x", 0): None, ("x", 1): gx < count_x - 1,
@@ -140,20 +145,11 @@
     for d in ORDER:
         for to in (z_peer((ma + d) % GROUP), y_peer((y + d) % GROUP), xc_peer((xc + d) % GROUP)):
             pl.semaphore_signal(barrier, inc=1, device_id=to, device_id_type=MESH)
-    copy_spectra.start()
-    copy_load.start()
-    copy_prof.start()
 
     copy_spectra.wait()
     ones = jnp.ones((8, nm), BF16)
     for x in range(nx):
         sums_own[x:x + 1, :] = dot(ones, ext[RADIUS + x, SIDE:SIDE + ny, :], NT)[0:1, :]
-    at = lax.broadcasted_iota(jnp.int32, (2 * nx, 16 * nx), 0)
-    column = lax.broadcasted_iota(jnp.int32, (2 * nx, 16 * nx), 1)
-    for side, first in ((0, SIDE), (1, SIDE + ny - 16)):
-        tile = ext[RADIUS:RADIUS + nx, first:first + 16, :].reshape(16 * nx, nm)
-        pick = column == 16 * (at >> 1) + (at & 1) + side * (16 - RADIUS)
-        edge_own[side] = dot(jnp.where(pick, 1.0, 0.0).astype(BF16), tile, NN).astype(BF16)
 
     near_x = (gx > 0).astype(jnp.int32) + (gx < count_x - 1).astype(jnp.int32)
     near_y = (gy > 0).astype(jnp.int32) + (gy < count_y - 1).astype(jnp.int32)
@@ -169,11 +165,22 @@
             device_id_type=MESH,
         )
 
-    for make in (sums, halo):
+    def start(make, chosen):
         for i, (dx, dy) in enumerate(steps):
-            @pl.when(exists(dx, dy))
-            def _():
-                make(i, dx, dy).start()
+            if chosen(dy):
+                @pl.when(exists(dx, dy))
+                def _():
+                    make(i, dx, dy).start()
+
+    start(sums, lambda dy: True)
+    start(halo, lambda dy: dy == 0)
+    at = lax.broadcasted_iota(jnp.int32, (2 * nx, 16 * nx), 0)
+    column = lax.broadcasted_iota(jnp.int32, (2 * nx, 16 * nx), 1)
+    for side, first in ((0, SIDE), (1, SIDE + ny - 16)):
+        tile = ext[RADIUS:RADIUS + nx, first:first + 16, :].reshape(16 * nx, nm)
+        pick = column == 16 * (at >> 1) + (at & 1) + side * (16 - RADIUS)
+        edge_own[side] = dot(jnp.where(pick, 1.0, 0.0).astype(BF16), tile, NN).astype(BF16)
+    start(halo, lambda dy: dy != 0)
 
     def copy(stage, source, target, device, recv=None):
         return pltpu.make_async_remote_copy(
@@ -333,10 +340,11 @@
         part = both[0:32] + both[32:64] + dot(prof_hi, clean_lo[i], NT)
         part_send[:, 2 * i, :] = part[:, 0:ny]
         part_send[:, 2 * i + 1, :] = part[:, ny:2 * ny]
-    for c in range(own):
+    for c in range(CHUNKS):
         for d in ORDER:
             p = (ma + d) % GROUP
-            copy(6, part_send.at[own * p + c], part_all.at[c, d - 1], z_peer(p), part_recv.at[c]).start()
+            source = part_send.at[pl.ds(own * p + size * c, size)]
+            copy(6, source, part_all.at[c, d - 1], z_peer(p), part_recv.at[c]).start()
         if c == 0:
             gram_c[ma] = pack_gram(dot(new_prof, jnp.concatenate([new_prof] * 4, axis=0), NT, HIGH))
             exchange(7, ma, z_peer, lambda p: gram_c.at[ma], gram_c)
@@ -354,20 +362,27 @@
         below_all[:, 2 * i, :] = below[:, 0:ny]
         below_all[:, 2 * i + 1, :] = below[:, ny:2 * ny]
 
-    for c in range(own):
+    for c in range(CHUNKS):
         whole = part_all.at[c]
         copy(6, whole, whole, z_peer((ma + 1) % GROUP), part_recv.at[c]).wait_recv()
-        k = own * ma + c
-        value = part_send[k]
+        k = own * ma + size * c
+        value = part_send[pl.ds(k, size)]
         for d in range(GROUP - 1):
             value = value + part_all[c, d]
-        new_all[c] = load_in[k] * value / below_all[own * (ma % 2) + c]
+        below = below_all[pl.ds(own * (ma % 2) + size * c, size)]
+        new_all[c] = load_in[pl.ds(k, size)] * value / below
         for p in range(GROUP):
             @pl.when(ma != p)
             def _():
-                copy(8, new_all.at[c], out_load.at[k], z_peer(p)).start()
-    copy_mine = pltpu.make_async_copy(new_all, out_load.at[pl.ds(own * ma, own)], local_sem.at[4])
-    copy_mine.start()
+                copy(8, new_all.at[c], out_load.at[pl.ds(k, size)], z_peer(p)).start()
+    mine = [
+        pltpu.make_async_copy(
+            new_all.at[c], out_load.at[pl.ds(own * ma + size * c, size)], local_sem.at[4 + c]
+        )
+        for c in range(CHUNKS)
+    ]
+    for part in mine:
+        part.start()
 
     for i, (dx, dy) in enumerate(steps):
         @pl.when(exists(dx, dy))
@@ -384,7 +399,8 @@
     peer = z_peer((ma + 1) % GROUP)
     copy(6, part_all, part_all, peer).wait_send()
     copy_new.wait()
-    copy_mine.wait()
+    for part in mine:
+        part.wait()
     most = out_load.at[0:nk - own]
     copy(8, most, most, peer).wait_send()
     copy(8, most, most, peer).wait_recv()
@@ -434,22 +450,22 @@
             vmem((nk, nm), F32),
             vmem((GROUP, 8, 128), F32),
             vmem((nk, nx, ny), F32),
-            vmem((own, GROUP - 1, nx, ny), F32),
+            vmem((CHUNKS, GROUP - 1, own // CHUNKS, nx, ny), F32),
             vmem((8, nx, ny), F32),
-            vmem((own, nx, ny), F32),
+            vmem((CHUNKS, own // CHUNKS, nx, ny), F32),
             vmem((128, 128), F32),
             vmem((nx, ny), F32),
             vmem((8, nx, ny), F32),
             vmem((2, 2 * nx, nm), BF16),
             vmem((2, 2 * nx + 32, nm), BF16),
-            pltpu.SemaphoreType.DMA((5,)),
+            pltpu.SemaphoreType.DMA((4 + CHUNKS,)),
             pltpu.SemaphoreType.DMA((8,)),
             pltpu.SemaphoreType.DMA((8,)),
             pltpu.SemaphoreType.DMA((8,)),
             pltpu.SemaphoreType.DMA((8,)),
             pltpu.SemaphoreType.DMA((9,)),
             pltpu.SemaphoreType.DMA((9,)),
-            pltpu.SemaphoreType.DMA((own,)),
+            pltpu.SemaphoreType.DMA((CHUNKS,)),
         ],
         compiler_params=pltpu.CompilerParams(
             collective_id=0, has_side_effects=True, vmem_limit_bytes=60 * 1024 * 1024

time: 55.6 us -> 54.6 us (0.982)
  Pallas kernels: 54.8 us -> 53.9 us
    pallas_call x1, Pallas kernels: 54.1 us -> 53.1 us  [per_device(): pl.pallas_call(kernel, out_shape=(pltpu.VMEM((nk, nx, ny), F32), pltpu.VM...]
where the time goes in v4:
time: 54.6 us; the launch traced here: 54.5 us
  Pallas kernels  53.9 us (99%)
  between operations  0.64 us (1%)
    pallas_call x1, Pallas kernels, per_device(): pl.pallas_call(kernel, out_shape=(pltpu.VMEM((nk, nx, ny), F32), pltpu.VM...  53.1 us

profile of v4, /device:TPU:1, one launch (start us, length us, event | category | flops | bytes accessed | tf_op | source)
XLA Modules:
  0.0 54.5 jit_solution(9387330298013003795)
XLA Ops:
  0.6 53.1 %shard_map.50 = (f32[32,16,128]{2,1,0:T(8,128)S(1)}, f32[32,256]{1,0:T(8,128)S(1)}) custom-call(bf16[16,128,256]{2,1,0:T(8,128)(2,1)} %spectra.1, f32[32,16,128]{2,1,0:T(8,128)} %loadings.1, f32[32,256]{1,0:T(8,128)} %profiles.1), custom_call_target="tpu_custom_call" | custom-call | tf_op jit(solution)/shard_map/pallas_call | solution.py:424
  53.8 0.7 %shard_map.51 = (f32[32,16,128]{2,1,0:T(8,128)}, f32[32,256]{1,0:T(8,128)}) custom-call(f32[32,16,128]{2,1,0:T(8,128)S(1)} %get-tuple-element.4.load, f32[32,256]{1,0:T(8,128)S(1)} %get-tuple-element.5.prof), custom_call_target="tpu_custom_call" | custom-call | tf_op jit(solution)/shard_map/pallas_call | solution.py:474

commit v5 on v4

--- a/solution.py
+++ b/solution.py
@@ -69,7 +69,7 @@
     ext, load_in, prof_in, ysm, smooth, rows, load_flat, load_split, clean_hi, clean_lo,
     bg_all, gram_a, gram_b, prof_send, prof_1, prof_2, prof_3, prof_new,
     gram_c, part_send, part_all, below_all, new_all, pad_t,
-    sums_own, sums_in, edge_own, edge_in, local_sem, sums_send, sums_recv, halo_send, halo_recv, send_sem, recv_sem, part_recv,
+    band_bg, sums_own, sums_in, edge_own, edge_in, local_sem, sums_send, sums_recv, halo_send, halo_recv, send_sem, recv_sem, part_recv, heard,
 ):
     nx, ny, nm = spectra.shape
     nk = loadings.shape[0]
@@ -143,7 +143,9 @@
                 barrier, inc=1, device_id={"gx": gx + dx, "gy": gy + dy, "ma": ma}, device_id_type=MESH
             )
     for d in ORDER:
-        for to in (z_peer((ma + d) % GROUP), y_peer((y + d) % GROUP), xc_peer((xc + d) % GROUP)):
+        far = d == GROUP // 2
+        near = () if far else (z_peer((ma + d) % GROUP), y_peer((y + d) % GROUP))
+        for to in (*near, xc_peer((xc + d) % GROUP)):
             pl.semaphore_signal(barrier, inc=1, device_id=to, device_id_type=MESH)
 
     copy_spectra.wait()
@@ -151,9 +153,13 @@
     for x in range(nx):
         sums_own[x:x + 1, :] = dot(ones, ext[RADIUS + x, SIDE:SIDE + ny, :], NT)[0:1, :]
 
+    hi_taps = weights.astype(ml_dtypes.bfloat16).astype(np.float32)
+    lo_taps = (weights - hi_taps).astype(ml_dtypes.bfloat16).astype(np.float32)
+    band_bg[...] = band((ny, 3 * ny), ny, hi_taps + lo_taps)
+
     near_x = (gx > 0).astype(jnp.int32) + (gx < count_x - 1).astype(jnp.int32)
     near_y = (gy > 0).astype(jnp.int32) + (gy < count_y - 1).astype(jnp.int32)
-    pl.semaphore_wait(barrier, 3 * (GROUP - 1) + near_x + near_y + near_x * near_y)
+    pl.semaphore_wait(barrier, 3 * (GROUP - 1) - 2 + near_x + near_y + near_x * near_y)
 
     def sums(i, dx, dy):
         return pltpu.make_async_remote_copy(
@@ -173,6 +179,9 @@
                     make(i, dx, dy).start()
 
     start(sums, lambda dy: True)
+    before_y, before_z = y_peer((y + GROUP - 1) % GROUP), z_peer((ma + GROUP - 1) % GROUP)
+    for sem, to in ((0, before_y), (1, before_z)):
+        pl.semaphore_signal(heard.at[sem], inc=1, device_id=to, device_id_type=MESH)
     start(halo, lambda dy: dy == 0)
     at = lax.broadcasted_iota(jnp.int32, (2 * nx, 16 * nx), 0)
     column = lax.broadcasted_iota(jnp.int32, (2 * nx, 16 * nx), 1)
@@ -247,20 +256,19 @@
         rows[RADIUS:nx + RADIUS, columns] = sums_own[...] if side == 0 else sums_in[steps.index((0, -side))]
         rows[nx + RADIUS:nx + 2 * RADIUS, columns] = sums_in[high, 0:RADIUS, :]
 
-    hi_taps = weights.astype(ml_dtypes.bfloat16).astype(np.float32)
-    lo_taps = (weights - hi_taps).astype(ml_dtypes.bfloat16).astype(np.float32)
     wide = (ny, ny + 2 * SIDE)
-    both_taps = hi_taps + lo_taps
     w0, w1, w2 = (float(weights[RADIUS + a]) for a in range(3))
     row_x = (
         w0 * rows[2:nx + 2, :] + w1 * (rows[1:nx + 1, :] + rows[3:nx + 3, :])
         + w2 * (rows[0:nx, :] + rows[4:nx + 4, :])
     )
-    bg_all[ma] = dot(row_x, band((ny, 3 * ny), ny, both_taps), NT, HIGH)
+    bg_all[ma] = dot(row_x, band_bg[...], NT, HIGH)
+    pl.semaphore_wait(heard.at[1], 1)
     exchange(1, ma, z_peer, lambda p: bg_all.at[ma], bg_all)
 
     arrive(0, xc, xc_peer, gram_a)
     gram_b[y] = total(gram_a)
+    pl.semaphore_wait(heard.at[0], 1)
     exchange(2, y, y_peer, lambda p: gram_b.at[y], gram_b)
     band_two = jnp.concatenate(
         [band(wide, SIDE, hi_taps), band(wide, SIDE, lo_taps)], axis=0
@@ -454,6 +462,7 @@
             vmem((8, nx, ny), F32),
             vmem((CHUNKS, own // CHUNKS, nx, ny), F32),
             vmem((128, 128), F32),
+            vmem((ny, 3 * ny), F32),
             vmem((nx, ny), F32),
             vmem((8, nx, ny), F32),
             vmem((2, 2 * nx, nm), BF16),
@@ -466,6 +475,7 @@
             pltpu.SemaphoreType.DMA((9,)),
             pltpu.SemaphoreType.DMA((9,)),
             pltpu.SemaphoreType.DMA((CHUNKS,)),
+            pltpu.SemaphoreType.REGULAR((2,)),
         ],
         compiler_params=pltpu.CompilerParams(
             collective_id=0, has_side_effects=True, vmem_limit_bytes=60 * 1024 * 1024

time: 54.6 us -> 54 us (0.989); the launches traced: 54.5 us -> 53.3 us
  Pallas kernels: 53.9 us -> 52.7 us
    pallas_call x1, Pallas kernels: 53.1 us -> 51.9 us  [per_device(): pl.pallas_call(kernel, out_shape=(pltpu.VMEM((nk, nx, ny), F32), pltpu.VM...]
where the time goes in v5:
time: 54 us; the launch traced here: 53.3 us
  Pallas kernels  52.7 us (98%)
  between operations  0.64 us (1%)
    pallas_call x1, Pallas kernels, per_device(): pl.pallas_call(kernel, out_shape=(pltpu.VMEM((nk, nx, ny), F32), pltpu.VM...  51.9 us

profile of v5, /device:TPU:1, one launch (start us, length us, event | category | flops | bytes accessed | tf_op | source)
XLA Modules:
  0.0 53.3 jit_solution(16931199605334487941)
XLA Ops:
  0.6 51.9 %shard_map.50 = (f32[32,16,128]{2,1,0:T(8,128)S(1)}, f32[32,256]{1,0:T(8,128)S(1)}) custom-call(bf16[16,128,256]{2,1,0:T(8,128)(2,1)} %spectra.1, f32[32,16,128]{2,1,0:T(8,128)} %loadings.1, f32[32,256]{1,0:T(8,128)} %profiles.1), custom_call_target="tpu_custom_call" | custom-call | tf_op jit(solution)/shard_map/pallas_call | solution.py:432
  52.6 0.7 %shard_map.51 = (f32[32,16,128]{2,1,0:T(8,128)}, f32[32,256]{1,0:T(8,128)}) custom-call(f32[32,16,128]{2,1,0:T(8,128)S(1)} %get-tuple-element.4.load, f32[32,256]{1,0:T(8,128)S(1)} %get-tuple-element.5.prof), custom_call_target="tpu_custom_call" | custom-call | tf_op jit(solution)/shard_map/pallas_call | solution.py:484

commit v6 on v5

--- a/solution.py
+++ b/solution.py
@@ -379,10 +379,8 @@
             value = value + part_all[c, d]
         below = below_all[pl.ds(own * (ma % 2) + size * c, size)]
         new_all[c] = load_in[pl.ds(k, size)] * value / below
-        for p in range(GROUP):
-            @pl.when(ma != p)
-            def _():
-                copy(8, new_all.at[c], out_load.at[pl.ds(k, size)], z_peer(p)).start()
+        for d in ORDER:
+            copy(8, new_all.at[c], out_load.at[pl.ds(k, size)], z_peer((ma + d) % GROUP)).start()
     mine = [
         pltpu.make_async_copy(
             new_all.at[c], out_load.at[pl.ds(own * ma + size * c, size)], local_sem.at[4 + c]

time: 54 us -> 54.9 us (1.017); the launches traced: 53.3 us -> 54.8 us
  Pallas kernels: 52.7 us -> 54.1 us
    pallas_call x1, Pallas kernels: 51.9 us -> 53.4 us  [per_device(): pl.pallas_call(kernel, out_shape=(pltpu.VMEM((nk, nx, ny), F32), pltpu.VM...]
where the time goes in v6:
time: 54.9 us; the launch traced here: 54.8 us
  Pallas kernels  54.1 us (99%)
  between operations  0.64 us (1%)
    pallas_call x1, Pallas kernels, per_device(): pl.pallas_call(kernel, out_shape=(pltpu.VMEM((nk, nx, ny), F32), pltpu.VM...  53.4 us

profile of v6, /device:TPU:1, one launch (start us, length us, event | category | flops | bytes accessed | tf_op | source)
XLA Modules:
  0.0 54.8 jit_solution(3824827043927614228)
XLA Ops:
  0.6 53.4 %shard_map.50 = (f32[32,16,128]{2,1,0:T(8,128)S(1)}, f32[32,256]{1,0:T(8,128)S(1)}) custom-call(bf16[16,128,256]{2,1,0:T(8,128)(2,1)} %spectra.1, f32[32,16,128]{2,1,0:T(8,128)} %loadings.1, f32[32,256]{1,0:T(8,128)} %profiles.1), custom_call_target="tpu_custom_call" | custom-call | tf_op jit(solution)/shard_map/pallas_call | solution.py:430
  54.0 0.7 %shard_map.51 = (f32[32,16,128]{2,1,0:T(8,128)}, f32[32,256]{1,0:T(8,128)}) custom-call(f32[32,16,128]{2,1,0:T(8,128)S(1)} %get-tuple-element.4.load, f32[32,256]{1,0:T(8,128)S(1)} %get-tuple-element.5.prof), custom_call_target="tpu_custom_call" | custom-call | tf_op jit(solution)/shard_map/pallas_call | solution.py:482

commit v7 on v5

--- a/solution.py
+++ b/solution.py
@@ -73,7 +73,7 @@
 ):
     nx, ny, nm = spectra.shape
     nk = loadings.shape[0]
-    size = nk // GROUP // CHUNKS
+    size = nx // CHUNKS
     own = nk // GROUP
     gx, gy, ma = lax.axis_index("gx"), lax.axis_index("gy"), lax.axis_index("ma")
     count_x, count_y = lax.axis_size("gx"), lax.axis_size("gy")
@@ -343,15 +343,15 @@
 
     prof_hi, prof_lo = split(new_prof)
     prof_two = jnp.concatenate([prof_hi, prof_lo], axis=0)
-    for i in range(nx // 2):
-        both = dot(prof_two, clean_hi[i], NT)
-        part = both[0:32] + both[32:64] + dot(prof_hi, clean_lo[i], NT)
-        part_send[:, 2 * i, :] = part[:, 0:ny]
-        part_send[:, 2 * i + 1, :] = part[:, ny:2 * ny]
     for c in range(CHUNKS):
+        for i in range(c * size // 2, (c + 1) * size // 2):
+            both = dot(prof_two, clean_hi[i], NT)
+            part = both[0:32] + both[32:64] + dot(prof_hi, clean_lo[i], NT)
+            part_send[c, :, 2 * i - c * size, :] = part[:, 0:ny]
+            part_send[c, :, 2 * i + 1 - c * size, :] = part[:, ny:2 * ny]
         for d in ORDER:
             p = (ma + d) % GROUP
-            source = part_send.at[pl.ds(own * p + size * c, size)]
+            source = part_send.at[c, pl.ds(own * p, own)]
             copy(6, source, part_all.at[c, d - 1], z_peer(p), part_recv.at[c]).start()
         if c == 0:
             gram_c[ma] = pack_gram(dot(new_prof, jnp.concatenate([new_prof] * 4, axis=0), NT, HIGH))
@@ -373,19 +373,20 @@
     for c in range(CHUNKS):
         whole = part_all.at[c]
         copy(6, whole, whole, z_peer((ma + 1) % GROUP), part_recv.at[c]).wait_recv()
-        k = own * ma + size * c
-        value = part_send[pl.ds(k, size)]
+        k = own * ma
+        band_x = slice(size * c, size * (c + 1))
+        value = part_send[c, pl.ds(k, own)]
         for d in range(GROUP - 1):
             value = value + part_all[c, d]
-        below = below_all[pl.ds(own * (ma % 2) + size * c, size)]
-        new_all[c] = load_in[pl.ds(k, size)] * value / below
+        below = below_all[pl.ds(own * (ma % 2), own), band_x, :]
+        new_all[c] = load_in[pl.ds(k, own), band_x, :] * value / below
         for p in range(GROUP):
             @pl.when(ma != p)
             def _():
-                copy(8, new_all.at[c], out_load.at[pl.ds(k, size)], z_peer(p)).start()
+                copy(8, new_all.at[c], out_load.at[pl.ds(k, own), band_x, :], z_peer(p)).start()
     mine = [
         pltpu.make_async_copy(
-            new_all.at[c], out_load.at[pl.ds(own * ma + size * c, size)], local_sem.at[4 + c]
+            new_all.at[c], out_load.at[pl.ds(own * ma, own), size * c:size * (c + 1), :], local_sem.at[4 + c]
         )
         for c in range(CHUNKS)
     ]
@@ -457,10 +458,10 @@
             vmem((GROUP, 8, 128), F32),
             vmem((nk, nm), F32),
             vmem((GROUP, 8, 128), F32),
-            vmem((nk, nx, ny), F32),
-            vmem((CHUNKS, GROUP - 1, own // CHUNKS, nx, ny), F32),
+            vmem((CHUNKS, nk, nx // CHUNKS, ny), F32),
+            vmem((CHUNKS, GROUP - 1, own, nx // CHUNKS, ny), F32),
             vmem((8, nx, ny), F32),
-            vmem((CHUNKS, own // CHUNKS, nx, ny), F32),
+            vmem((CHUNKS, own, nx // CHUNKS, ny), F32),
             vmem((128, 128), F32),
             vmem((ny, 3 * ny), F32),
             vmem((nx, ny), F32),

time: 54 us -> 53.7 us (level)
  no operation moved by 1% of the time
where the time goes in v7:
time: 53.7 us; the launch traced here: 53.1 us
  Pallas kernels  52.4 us (98%)
  between operations  0.64 us (1%)
    pallas_call x1, Pallas kernels, per_device(): pl.pallas_call(kernel, out_shape=(pltpu.VMEM((nk, nx, ny), F32), pltpu.VM...  51.7 us

profile of v7, /device:TPU:1, one launch (start us, length us, event | category | flops | bytes accessed | tf_op | source)
XLA Modules:
  0.0 53.1 jit_solution(13684562540170433752)
XLA Ops:
  0.6 51.7 %shard_map.50 = (f32[32,16,128]{2,1,0:T(8,128)S(1)}, f32[32,256]{1,0:T(8,128)S(1)}) custom-call(bf16[16,128,256]{2,1,0:T(8,128)(2,1)} %spectra.1, f32[32,16,128]{2,1,0:T(8,128)} %loadings.1, f32[32,256]{1,0:T(8,128)} %profiles.1), custom_call_target="tpu_custom_call" | custom-call | tf_op jit(solution)/shard_map/pallas_call | solution.py:433
  52.3 0.7 %shard_map.51 = (f32[32,16,128]{2,1,0:T(8,128)}, f32[32,256]{1,0:T(8,128)}) custom-call(f32[32,16,128]{2,1,0:T(8,128)S(1)} %get-tuple-element.4.load, f32[32,256]{1,0:T(8,128)S(1)} %get-tuple-element.5.prof), custom_call_target="tpu_custom_call" | custom-call | tf_op jit(solution)/shard_map/pallas_call | solution.py:485
